TPU v7x, 256 devices: a whole 4x4x8 slice. The times are simulated.
256 devices in a mesh: gx: 4 (over y_lo, core), gy: 8 (over z), band: 8 (over y_hi, x).
Axes of the slice: x: 4, y: 4 (y_hi: 2, y_lo: 2; y = y_hi * 2 + y_lo), z: 8, core: 2. Of those that a mesh axis runs over, the one named last changes fastest.
Arguments:
- orbitals: bfloat16 [1152, 32, 16, 128], P('band', 'gx', 'gy'), may hold values from -6 to 6
- potential: float32 [32, 16, 128], P('gx', 'gy'), may hold values from -3 to 0.5
- panels: bfloat16 [2, 1152, 32, 16, 128], P(None, 'band', 'gx', 'gy'), may hold values from -6 to 6
Outputs:
- filtered: bfloat16 [1152, 32, 16, 128], P('band', 'gx', 'gy')
- margin: float32 [2, 1152, 1152], P(None, 'band', ('gx', 'gy'))
All inputs are finite; a program needn't handle non-finite values.
Results may differ from a plain program's by a relative error of at most 0.0034.
Values may be sent and summed in bfloat16 or wider, within the bound.
A program may use at most 64 MiB of HBM per device.

v0:
```python
import math

import jax
import jax.numpy as jnp
from jax import lax
from jax.sharding import PartitionSpec as P

filter_center = 13.0
filter_half = 12.0


def with_halo(x, sides, width):
    for axis, dim in sides:
        size, length = (lax.axis_size(axis), x.shape[dim])
        up = [(i, (i + 1) % size) for i in range(size)]
        down = [(j, i) for i, j in up]
        last = lax.slice_in_dim(x, length - width, length, axis=dim)
        initial = lax.slice_in_dim(x, 0, width, axis=dim)
        before = lax.ppermute(last, axis, up)
        after = lax.ppermute(initial, axis, down)
        x = jnp.concatenate([before, x, after], axis=dim)
    return x


def apply_hamiltonian(padded, potential):
    center = padded[:, 1:-1, 1:-1]
    neighbours = padded[:, 2:, 1:-1] + padded[:, :-2, 1:-1]
    neighbours = neighbours + padded[:, 1:-1, 2:] + padded[:, 1:-1, :-2]
    neighbours = neighbours + jnp.roll(center, -1, 3) + jnp.roll(center, 1, 3)
    return 2.0 * (6.0 * center - neighbours) + potential[None] * center


def widen(source):
    return with_halo(source, (("gx", 1), ("gy", 2)), 1)


def body(orbitals, potential, panels):
    values = orbitals.astype(jnp.float32)
    first_section = (
        (apply_hamiltonian(widen(orbitals).astype(jnp.float32), potential) - filter_center * values)
        / filter_half
    ).astype(jnp.bfloat16)
    stored = first_section.astype(jnp.float32)
    applied = apply_hamiltonian(widen(first_section).astype(jnp.float32), potential)
    filtered = (2.0 * (applied - filter_center * stored) / filter_half - values).astype(
        jnp.bfloat16
    )
    cell_total = (
        filtered.shape[1]
        * lax.axis_size("gx")
        * filtered.shape[2]
        * lax.axis_size("gy")
        * filtered.shape[3]
    )
    scale_factor = 1.0 / math.sqrt(cell_total)
    panel_count = panels.shape[0]
    own_bands = panels.shape[1]
    local_cells = panels.shape[2] * panels.shape[3] * panels.shape[4]
    panel_rows = panels.reshape(panel_count * own_bands, local_cells)
    block_piece = lax.all_gather(filtered, "band", axis=0, tiled=True)
    flat_piece = block_piece.reshape(block_piece.shape[0], local_cells)
    product = lax.dot_general(
        panel_rows, flat_piece, (((1,), (1,)), ((), ())), preferred_element_type=jnp.float32
    )
    partial_terms = product.reshape(panel_count, own_bands, block_piece.shape[0])
    totals = lax.psum(partial_terms, ("gx", "gy"))
    share = totals.shape[2] // (lax.axis_size("gx") * lax.axis_size("gy"))
    summed = lax.dynamic_slice_in_dim(totals, lax.axis_index(("gx", "gy")) * share, share, 2)
    margin = summed * scale_factor
    return (filtered, margin)


def solution(mesh):
    return jax.shard_map(
        body,
        mesh=mesh,
        in_specs=(
            P("band", "gx", "gy", None),
            P("gx", "gy", None),
            P(None, "band", "gx", "gy", None),
        ),
        out_specs=(P("band", "gx", "gy", None), P(None, "band", ("gx", "gy"))),
        check_vma=False,
    )
```

profile of v0, /device:TPU:96, one launch (start us, length us, event | category | flops | bytes accessed | tf_op | source)
XLA Modules:
  0.0 385.6 jit_solution(15760880842293963004)
XLA Ops:
  7.2 1.0 fusion.23
  8.4 1.8 collective-permute-start.1
  10.2 1.9 collective-permute-done
  12.1 1.3 constant_dynamic-update-slice_fusion.1
  13.5 3.2 collective-permute-start.2
  16.7 8.5 %collective-permute-done.2 = bf16[144,10,1,128]{3,0,2,1:T(8,128)(2,1)S(1)} collective-permute-done((bf16[144,10,1,128]{3,0,2,1:T(8,128)(2,1)S(1)}, bf16[144,10,1,128]{3,0,2,1:T(8,128)(2,1)S(1)}, u32[]{:S(2)}, u32[]{:S(2)}) %collective-permute-start.2) | collective-permute-done | bytes 368672 | tf_op jit(solution)/shard_map/ppermute | solution.py:19
  25.2 3.4 collective-permute-done.3
  28.6 0.2 maximum_convert_fusion
  28.8 0.4 fusion.18
  29.2 0.4 fusion.19
  29.6 0.7 copy-done
  30.3 1.0 fusion.2
  31.4 1.7 collective-permute-start.5
  33.1 2.1 collective-permute-done.4
  35.4 0.4 collective-permute-start.6
  35.8 1.7 collective-permute-start.7
  37.5 9.0 %collective-permute-done.6 = bf16[144,10,1,128]{3,0,2,1:T(8,128)(2,1)S(1)} collective-permute-done((bf16[144,10,1,128]{3,0,2,1:T(8,128)(2,1)S(1)}, bf16[144,10,1,128]{3,0,2,1:T(8,128)(2,1)S(1)}, u32[]{:S(2)}, u32[]{:S(2)}) %collective-permute-start.6) | collective-permute-done | bytes 368672 | tf_op jit(solution)/shard_map/ppermute | solution.py:19
  46.5 1.3 collective-permute-done.7
  47.8 0.3 maximum_convert_fusion.1
  48.1 0.4 fusion.16
  48.5 0.4 fusion.17
  48.9 1.1 fusion.3
  50.0 1.0 copy.17
  51.1 0.2 all-reduce.2.cloned.1.call-start
  51.5 0.9 reshape.15
  52.4 79.1 %all-gather.2.cloned.1.call-done = bf16[1152,8,2,128]{3,1,2,0:T(8,128)(2,1)} async-done(((bf16[144,8,2,128]{3,1,2,0:T(8,128)(2,1)}), bf16[1152,8,2,128]{3,1,2,0:T(8,128)(2,1)}) %all-gather.2.cloned.1.call-update) | async-done | bytes 4718608 | tf_op jit(solution)/shard_map/all_gather | solution.py:60
  131.5 7.1 %copy.18 = bf16[1152,8,2,128]{0,3,2,1:T(8,128)(2,1)} copy(bf16[1152,8,2,128]{3,1,2,0:T(8,128)(2,1)} %all-gather.2.cloned.1.call-done) | data formatting | bytes 9437184 | tf_op jit(solution)/shard_map/all_gather | solution.py:60
  138.6 4.0 %fusion.24 = f32[1152,288]{0,1:T(8,128)S(1)} fusion(bf16[288,2048]{1,0:T(8,128)(2,1)S(1)} %reshape.15, bf16[1152,2048]{0,1:T(8,128)(2,1)} %bitcast.6), kind=kOutput, calls=%fused_computation.39 | convolution fusion | flops 1358954496 | bytes 7225344 | tf_op jit(solution)/shard_map/dot_general | solution.py:62
  142.6 3.1 copy.19
  145.7 1.3 copy.20
  147.0 230.2 %all-reduce.2.cloned.1.call-done = f32[2,144,1152]{1,0,2:T(2,128)} async-done(((f32[2,144,1152]{1,0,2:T(2,128)}), f32[2,144,1152]{1,0,2:T(2,128)}) %all-reduce.2.cloned.1.call-update) | async-done | bytes 1327120 | tf_op jit(solution)/shard_map/psum | solution.py:66
  377.2 1.5 dynamic-slice_multiply_fusion
  (21 shorter events, 0.7 us)
Async XLA Ops:
  7.2 124.3 %all-gather.2.cloned.1.call-start = ((), (), s32[]{:S(2)}) async-start(), calls=%async_computation | async-start | bytes 5308416 | tf_op jit(solution)/shard_map/all_gather | solution.py:60
  8.3 3.9 collective-permute-start
  8.4 5.0 %collective-permute-start.1 = (bf16[144,1,2,128]{3,0,2,1:T(8,128)(2,1)S(1)}, bf16[144,1,2,128]{3,0,2,1:T(8,128)(2,1)S(1)}, u32[]{:S(2)}, u32[]{:S(2)}) collective-permute-start(bf16[144,1,2,128]{3,0,2,1:T(8,128)(2,1)S(1)} %copy.25), channel_id=1, source_target_pairs={{64,0},{128,64},{192,128},{0,192},{65,1},{129,65},{193,129},{1,193... | collective-permute-start | bytes 221192 | tf_op jit(solution)/shard_map/ppermute | solution.py:20
  13.5 11.7 %collective-permute-start.2 = (bf16[144,10,1,128]{3,0,2,1:T(8,128)(2,1)S(1)}, bf16[144,10,1,128]{3,0,2,1:T(8,128)(2,1)S(1)}, u32[]{:S(2)}, u32[]{:S(2)}) collective-permute-start(bf16[144,10,1,128]{3,0,2,1:T(8,128)(2,1)S(1)} %get-tuple-element.16), channel_id=1, source_target_pairs={{0,8},{8,16},{16,24},{24,32},{32,40},{40,48},{48,56},{56,0},{1,9},... | collective-permute-start | bytes 1105928 | tf_op jit(solution)/shard_map/ppermute | solution.py:19
  16.7 11.9 %collective-permute-start.3 = (bf16[144,10,1,128]{3,0,2,1:T(8,128)(2,1)S(1)}, bf16[144,10,1,128]{3,0,2,1:T(8,128)(2,1)S(1)}, u32[]{:S(2)}, u32[]{:S(2)}) collective-permute-start(bf16[144,10,1,128]{3,0,2,1:T(8,128)(2,1)S(1)} %get-tuple-element.17), channel_id=1, source_target_pairs={{8,0},{16,8},{24,16},{32,24},{40,32},{48,40},{56,48},{0,56},{9,1},... | collective-permute-start | bytes 1105928 | tf_op jit(solution)/shard_map/ppermute | solution.py:20
  29.2 1.1 copy-start
  29.2 1.1 copy-start.2
  31.3 3.9 %collective-permute-start.4 = (bf16[144,1,2,128]{3,0,2,1:T(8,128)(2,1)S(1)}, bf16[144,1,2,128]{3,0,2,1:T(8,128)(2,1)S(1)}, u32[]{:S(2)}, u32[]{:S(2)}) collective-permute-start(bf16[144,1,2,128]{3,0,2,1:T(8,128)(2,1)S(1)} %get-tuple-element.18), channel_id=1, source_target_pairs={{0,64},{64,128},{128,192},{192,0},{1,65},{65,129},{129,193},{193,1... | collective-permute-start | bytes 221192 | tf_op jit(solution)/shard_map/ppermute | solution.py:19
  31.4 3.9 collective-permute-start.5
  35.4 11.1 %collective-permute-start.6 = (bf16[144,10,1,128]{3,0,2,1:T(8,128)(2,1)S(1)}, bf16[144,10,1,128]{3,0,2,1:T(8,128)(2,1)S(1)}, u32[]{:S(2)}, u32[]{:S(2)}) collective-permute-start(bf16[144,10,1,128]{3,0,2,1:T(8,128)(2,1)S(1)} %get-tuple-element.14), channel_id=1, source_target_pairs={{0,8},{8,16},{16,24},{24,32},{32,40},{40,48},{48,56},{56,0},{1,9},... | collective-permute-start | bytes 1105928 | tf_op jit(solution)/shard_map/ppermute | solution.py:19
  35.8 12.0 %collective-permute-start.7 = (bf16[144,10,1,128]{3,0,2,1:T(8,128)(2,1)S(1)}, bf16[144,10,1,128]{3,0,2,1:T(8,128)(2,1)S(1)}, u32[]{:S(2)}, u32[]{:S(2)}) collective-permute-start(bf16[144,10,1,128]{3,0,2,1:T(8,128)(2,1)S(1)} %get-tuple-element.15), channel_id=1, source_target_pairs={{8,0},{16,8},{24,16},{32,24},{40,32},{48,40},{56,48},{0,56},{9,1},... | collective-permute-start | bytes 1105928 | tf_op jit(solution)/shard_map/ppermute | solution.py:20
  50.0 1.5 copy-start.1
  51.1 326.1 %all-reduce.2.cloned.1.call-start = ((), (), s32[]{:S(2)}) async-start(), calls=%async_computation.1 | async-start | bytes 4718592 | tf_op jit(solution)/shard_map/psum | solution.py:66
Sparse Core Ops, SparseCore 0:
  51.2 80.2 all-gather.1
  145.8 231.2 all-reduce.1
where the time goes:
time: 390 us; the launch traced here: 386 us
  waiting for transfers between devices  336 us (86%)
  local copies, waits for them, and re-layouts  18.2 us (5%)
  between operations  14.2 us (4%)
  starting transfers between devices  9.27 us (2%)
  other arithmetic  4.25 us (1%)
  matrix products  4.02 us (1%)
    psum x1, waiting for transfers between devices, body(): totals = lax.psum(partial_terms, ('gx', 'gy'))  230 us
    all_gather x1, waiting for transfers between devices, body(): block_piece = lax.all_gather(filtered, 'band', axis=0, tiled=True)  79.1 us
    ppermute x4, waiting for transfers between devices, with_halo(): before = lax.ppermute(last, axis, up)  21.6 us
  transfers between devices with their start and end apart: 10, of which 8 were waited for; matrix products, arithmetic and copies ran while one was open for 1% of the time, Pallas kernels for 0%

commit v1 on v0

v1 whole, which is shorter than its diff:
```python
import functools
import math

import jax
import jax.numpy as jnp
from jax import lax
from jax.experimental import pallas as pl
from jax.experimental.pallas import tpu as pltpu
from jax.sharding import PartitionSpec as P

MESH = pl.DeviceIdType.MESH
NT = (((1,), (1,)), ((), ()))
CHUNKS = ((0, 48), (48, 64), (112, 32))


def kernel(
    scale,
    o_ref,
    pot_ref,
    p_ref,
    filt_ref,
    out_ref,
    potn,
    yb,
    xb,
    db,
    pan,
    first,
    fb,
    core_send,
    core_own,
    core_recv,
    y_send,
    y_recv,
    total,
    z_send,
    z_recv,
    halo_ss,
    halo_rs,
    pot_ss,
    pot_rs,
    pan_sem,
    own_sem,
    swap_ss,
    swap_rs,
    near_ss,
    near_rs,
    far_ss,
    far_rs,
    core_ss,
    core_rs,
    y_ss,
    y_rs,
    z_ss,
    z_rs,
):
    bf16, f32 = jnp.bfloat16, jnp.float32
    gx, gy, w = lax.axis_index("gx"), lax.axis_index("gy"), lax.axis_index("band")
    ylo, core = gx // 2, gx % 2
    yhi, xx = w // 4, w % 4
    ylo_other, core_other, yhi_other = 1 - ylo, 1 - core, 1 - yhi
    gx_prev, gx_next = (gx + 3) % 4, (gx + 1) % 4
    gy_prev, gy_next = (gy + 7) % 8, (gy + 1) % 8
    w_next, w_prev = yhi * 4 + (xx + 1) % 4, yhi * 4 + (xx + 3) % 4
    w_across = yhi_other * 4 + xx
    gx_core, gx_ylo = ylo * 2 + core_other, ylo_other * 2 + core

    barrier = pltpu.get_barrier_semaphore()
    partners = [(gx_prev, gy, w), (gx_next, gy, w)]
    partners += [(gx, (gy + d) % 8, w) for d in range(1, 8)]
    partners += [(a, b, w) for a in (gx_prev, gx_next) for b in (gy_prev, gy_next)]
    partners += [(gx, gy, w_across), (gx, gy, w_next), (gx, gy, w_prev)]
    partners += [(gx_ylo, gy, w), (gx_ylo, gy, w_across)]
    for device in partners:
        pl.semaphore_signal(barrier, 1, device_id=device, device_id_type=MESH)
    pl.semaphore_wait(barrier, len(partners))

    def remote(src, dst, ss, rs, device):
        return pltpu.make_async_remote_copy(
            src_ref=src, dst_ref=dst, send_sem=ss, recv_sem=rs, device_id=device, device_id_type=MESH
        )

    pending = []

    def start(copy):
        copy.start()
        pending.append(copy)
        return copy

    pots = [
        start(remote(pot_ref, potn.at[i], pot_ss.at[i], pot_rs.at[i], device))
        for i, device in enumerate(
            ((gx_next, gy, w), (gx_prev, gy, w), (gx, gy_next, w), (gx, gy_prev, w))
        )
    ]
    halos = []
    for k, (s0, n) in enumerate(CHUNKS):
        rows = pl.ds(s0, n)
        plan = (
            (o_ref.at[rows], yb.at[0, rows], (gx, gy_next, w)),
            (o_ref.at[rows], yb.at[1, rows], (gx, gy_prev, w)),
            (o_ref.at[rows, pl.ds(1536, 512)], xb.at[0, rows], (gx_next, gy, w)),
            (o_ref.at[rows, pl.ds(0, 512)], xb.at[1, rows], (gx_prev, gy, w)),
            (o_ref.at[rows, pl.ds(1920, 128)], db.at[0, rows], (gx_next, gy_next, w)),
            (o_ref.at[rows, pl.ds(1792, 128)], db.at[1, rows], (gx_next, gy_prev, w)),
            (o_ref.at[rows, pl.ds(128, 128)], db.at[2, rows], (gx_prev, gy_next, w)),
            (o_ref.at[rows, pl.ds(0, 128)], db.at[3, rows], (gx_prev, gy_prev, w)),
        )
        halos.append(
            [
                start(remote(src, dst, halo_ss.at[k, i], halo_rs.at[k, i], device))
                for i, (src, dst, device) in enumerate(plan)
            ]
        )
    mine, theirs = pl.ds(yhi * 1024, 1024), pl.ds(yhi_other * 1024, 1024)
    pan_own = pltpu.make_async_copy(p_ref.at[:, mine], pan.at[yhi], pan_sem.at[2])
    pan_own.start()
    pan_swap = start(
        remote(p_ref.at[:, theirs], pan.at[yhi], pan_sem.at[0], pan_sem.at[1], (gx, gy, w_across))
    )
    z_send[:, 32:48, :] = jnp.zeros((8, 16, z_send.shape[2]), bf16)

    def filter_rows(rows):
        def orb(x, y):
            if 0 <= x < 8:
                if y < 0:
                    piece = yb[0, rows, 128 * (2 * x + y + 2) : 128 * (2 * x + y + 3)]
                elif y > 1:
                    piece = yb[1, rows, 128 * (2 * x + y - 2) : 128 * (2 * x + y - 1)]
                else:
                    piece = o_ref[rows, 128 * (2 * x + y) : 128 * (2 * x + y + 1)]
            elif 0 <= y < 2:
                side, r = (0, 2 * (x + 2) + y) if x < 0 else (1, 2 * (x - 8) + y)
                piece = xb[side, rows, 128 * r : 128 * (r + 1)]
            else:
                piece = db[(0 if x < 0 else 2) + (0 if y < 0 else 1), rows, :]
            return piece.astype(f32)

        def slot(x, y):
            if 0 <= x < 8:
                return 2 * x + y if 0 <= y < 2 else (16 + x if y < 0 else 24 + x)
            return 32 + y if x < 0 else 34 + y

        def coefficient(x, y):
            if 0 <= x < 8 and 0 <= y < 2:
                p = pot_ref[2 * x + y : 2 * x + y + 1, :]
            elif y < 0:
                p = potn[2, 2 * x + 1 : 2 * x + 2, :]
            elif y > 1:
                p = potn[3, 2 * x : 2 * x + 1, :]
            elif x < 0:
                p = potn[0, 14 + y : 15 + y, :]
            else:
                p = potn[1, y : y + 1, :]
            return (p - 1.0) * (1.0 / 12.0)

        def both(v):
            return pltpu.roll(v, 1, 1) + pltpu.roll(v, 127, 1)

        cells = [(x, y) for x in range(8) for y in range(-1, 3)]
        cells += [(x, y) for x in (-1, 8) for y in (0, 1)]
        for x, y in cells:
            v = orb(x, y)
            s = orb(x + 1, y) + orb(x - 1, y) + orb(x, y + 1) + orb(x, y - 1) + both(v)
            first[slot(x, y)] = (coefficient(x, y) * v - s * (1.0 / 6.0)).astype(bf16).astype(f32)
        for x in range(8):
            for y in range(2):
                v = first[slot(x, y)]
                s = first[slot(x + 1, y)] + first[slot(x - 1, y)] + both(v)
                s = s + first[slot(x, y + 1)] + first[slot(x, y - 1)]
                value = 2.0 * coefficient(x, y) * v - s * (1.0 / 3.0) - orb(x, y)
                r = 2 * x + y
                filt_ref[rows, 128 * r : 128 * (r + 1)] = value.astype(bf16)

    swaps, owns, near, far = {}, {}, {}, {}
    cores, ys, zs = {}, {}, []

    def step_filter(k):
        s0, n = CHUNKS[k]
        if k == 0:
            for copy in pots:
                copy.wait_recv()
        for copy in halos[k]:
            copy.wait_recv()

        def sub(i, carry):
            filter_rows(pl.ds(pl.multiple_of(s0 + i * 16, 16), 16))
            return carry

        lax.fori_loop(0, n // 16, sub, 0)
        rows = pl.ds(s0, n)
        swaps[k] = start(
            remote(
                filt_ref.at[rows, theirs], fb.at[w, rows], swap_ss.at[k], swap_rs.at[k], (gx, gy, w_across)
            )
        )
        for d, to in enumerate((w_next, w_prev)):
            near[k, 0, d] = start(
                remote(
                    filt_ref.at[rows, mine],
                    fb.at[w, rows],
                    near_ss.at[k, 0, d],
                    near_rs.at[k, 0, d],
                    (gx, gy, to),
                )
            )
        owns[k] = pltpu.make_async_copy(filt_ref.at[rows, mine], fb.at[w, rows], own_sem.at[k])
        owns[k].start()

    def step_swap(k):
        s0, n = CHUNKS[k]
        rows = pl.ds(s0, n)
        swaps[k].wait_recv()
        for d, to in enumerate((w_next, w_prev)):
            near[k, 1, d] = start(
                remote(
                    fb.at[w_across, rows],
                    fb.at[w_across, rows],
                    near_ss.at[k, 1, d],
                    near_rs.at[k, 1, d],
                    (gx, gy, to),
                )
            )

    def step_forward(k, t):
        s0, n = CHUNKS[k]
        rows = pl.ds(s0, n)
        half = yhi if t == 0 else yhi_other
        for d, (to, origin) in enumerate(((w_next, (xx + 3) % 4), (w_prev, (xx + 1) % 4))):
            near[k, t, d].wait_recv()
            piece = fb.at[half * 4 + origin, rows, pl.ds(512 * d, 512)]
            far[k, t, d] = start(
                remote(piece, piece, far_ss.at[k, t, d], far_rs.at[k, t, d], (gx, gy, to))
            )

    def step_matmul(k):
        s0, n = CHUNKS[k]
        rows = pl.ds(s0, n)
        if k == 0:
            pan_own.wait()
            pan_swap.wait_recv()
        owns[k].wait()
        for t in range(2):
            for d in range(2):
                far[k, t, d].wait_recv()
        for side, dst in ((core_other, core_send), (core, core_own)):
            lhs = jnp.concatenate(
                [fb[4 * (q // 2) + 2 * side + q % 2, rows, :] for q in range(4)], axis=0
            )
            for rb in range(2):
                out = lax.dot_general(lhs, pan[rb], NT, preferred_element_type=f32) * scale
                for q in range(4):
                    dst[q // 2, q % 2, rb, rows, :] = out[n * q : n * (q + 1)]
            if dst is core_send:
                cores[k] = start(
                    remote(
                        core_send.at[:, :, :, rows],
                        core_recv.at[:, :, :, rows],
                        core_ss.at[k],
                        core_rs.at[k],
                        (gx_core, gy, w),
                    )
                )

    y_plan = (
        (ylo_other, yhi, (gx_ylo, gy, w)),
        (ylo, yhi_other, (gx, gy, w_across)),
        (ylo_other, yhi_other, (gx_ylo, gy, w_across)),
    )

    def step_core(k):
        s0, n = CHUNKS[k]
        rows = pl.ds(s0, n)
        cores[k].wait_recv()
        for j, (yl, yh, device) in enumerate(y_plan):
            for q in range(2):
                value = core_own[yl, q, yh, rows, :] + core_recv[yl, q, yh, rows, :]
                y_send[j, q, rows, :] = value.astype(bf16)
            ys[k, j] = start(
                remote(
                    y_send.at[j, :, rows], y_recv.at[j, :, rows], y_ss.at[k, j], y_rs.at[k, j], device
                )
            )
        for q in range(2):
            total[q, rows, :] = core_own[ylo, q, yhi, rows, :] + core_recv[ylo, q, yhi, rows, :]

    def step_y(k):
        s0, n = CHUNKS[k]
        rows = pl.ds(s0, n)
        for j in range(3):
            ys[k, j].wait_recv()
        for q in range(2):
            value = total[q, rows, :]
            for j in range(3):
                value = value + y_recv[j, q, rows, :].astype(f32)
            total[q, rows, :] = value
        done_before = s0 // 36
        for c in range(done_before, (s0 + n) // 36):
            for q in range(2):
                block = total[q, 36 * c : 36 * (c + 1), :]
                target = 4 * q + c

                @pl.when(target == gy)
                def _():
                    out_ref[0:36, :] = block

                @pl.when(target != gy)
                def _():
                    z_send[target, 0:36, :] = block.astype(bf16)
                    remote(
                        z_send.at[target], z_recv.at[gy], z_ss.at[target], z_rs.at[gy], (gx, target, w)
                    ).start()

    step_filter(0)
    step_swap(0)
    step_forward(0, 0)
    step_filter(1)
    step_forward(0, 1)
    step_swap(1)
    step_matmul(0)
    step_forward(1, 0)
    step_filter(2)
    step_forward(1, 1)
    step_swap(2)
    step_core(0)
    step_matmul(1)
    step_forward(2, 0)
    step_core(1)
    step_forward(2, 1)
    step_y(0)
    step_y(1)
    step_matmul(2)
    step_core(2)
    step_y(2)

    for s in range(8):

        @pl.when(s != gy)
        def _():
            copy = remote(z_send.at[s], z_recv.at[s], z_ss.at[s], z_rs.at[s], (gx, s, w))
            copy.wait_recv()
            out_ref[0:36, :] += z_recv[s, 0:36, :].astype(f32)
            copy.wait_send()

    for copy in pending:
        copy.wait_send()


def body(orbitals, potential, panels):
    bands, lx, ly, lz = orbitals.shape
    cells = lx * ly * lz
    panel_count = panels.shape[0]
    lines = panel_count * bands
    scale = 1.0 / math.sqrt(cells * lax.axis_size("gx") * lax.axis_size("gy"))
    bf16, f32 = jnp.bfloat16, jnp.float32
    c = len(CHUNKS)
    dma = pltpu.SemaphoreType.DMA
    filtered, sums = pl.pallas_call(
        functools.partial(kernel, scale),
        out_shape=(
            jax.ShapeDtypeStruct((bands, cells), bf16),
            jax.ShapeDtypeStruct((40, lines), f32),
        ),
        in_specs=[pl.BlockSpec(memory_space=pltpu.VMEM)] * 3,
        out_specs=(pl.BlockSpec(memory_space=pltpu.VMEM),) * 2,
        scratch_shapes=[
            pltpu.VMEM((4, lx * ly, lz), f32),
            pltpu.VMEM((2, bands, cells), bf16),
            pltpu.VMEM((2, bands, 512), bf16),
            pltpu.VMEM((4, bands, 128), bf16),
            pltpu.VMEM((2, lines, cells // 2), bf16),
            pltpu.VMEM((36, 16, 128), f32),
            pltpu.VMEM((8, bands, cells // 2), bf16),
            pltpu.VMEM((2, 2, 2, bands, lines), f32),
            pltpu.VMEM((2, 2, 2, bands, lines), f32),
            pltpu.VMEM((2, 2, 2, bands, lines), f32),
            pltpu.VMEM((3, 2, bands, lines), bf16),
            pltpu.VMEM((3, 2, bands, lines), bf16),
            pltpu.VMEM((2, bands, lines), f32),
            pltpu.VMEM((8, 48, lines), bf16),
            pltpu.VMEM((8, 48, lines), bf16),
            dma((c, 8)),
            dma((c, 8)),
            dma((4,)),
            dma((4,)),
            dma((3,)),
            dma((c,)),
            dma((c,)),
            dma((c,)),
            dma((c, 2, 2)),
            dma((c, 2, 2)),
            dma((c, 2, 2)),
            dma((c, 2, 2)),
            dma((c,)),
            dma((c,)),
            dma((c, 3)),
            dma((c, 3)),
            dma((8,)),
            dma((8,)),
        ],
        compiler_params=pltpu.CompilerParams(
            collective_id=0, has_side_effects=True, vmem_limit_bytes=48 << 20
        ),
        cost_estimate=pl.CostEstimate(
            flops=2 * lines * bands * 8 * cells, bytes_accessed=4 << 20, transcendentals=0
        ),
    )(
        orbitals.reshape(bands, cells),
        potential.reshape(lx * ly, lz),
        panels.reshape(lines, cells),
    )
    margin = sums[:36].T.reshape(panel_count, bands, 36)
    return filtered.reshape(orbitals.shape), margin


def solution(mesh):
    return jax.shard_map(
        body,
        mesh=mesh,
        in_specs=(
            P("band", "gx", "gy", None),
            P("gx", "gy", None),
            P(None, "band", "gx", "gy", None),
        ),
        out_specs=(P("band", "gx", "gy", None), P(None, "band", ("gx", "gy"))),
        check_vma=False,
    )
```

time: 390 us -> 75.4 us (0.19); the launches traced: 386 us -> 75.3 us
  waiting for transfers between devices: 336 us -> 0 us
  Pallas kernels: 0 us -> 67.3 us
  between operations: 14.2 us -> 0.67 us
  local copies, waits for them, and re-layouts: 18.2 us -> 7.25 us
  starting transfers between devices: 9.27 us -> 0 us
  other arithmetic: 4.25 us -> 0 us
  matrix products: 4.02 us -> 0 us
    psum x1 -> x0, waiting for transfers between devices: 230 us -> none  [body(): totals = lax.psum(partial_terms, ('gx', 'gy'))]
    all_gather x1 -> x0, waiting for transfers between devices: 79.1 us -> none  [body(): block_piece = lax.all_gather(filtered, 'band', axis=0, tiled=True)]
    pallas_call x0 -> x1, Pallas kernels: none -> 67.3 us  [body(): pl.pallas_call(functools.partial(kernel, scale), out_shape=(jax.ShapeDtyp...]
    ppermute x8 -> x0, waiting for transfers between devices: 26.3 us -> none  [the longest x4 21.6 us: with_halo(): before = lax.ppermute(last, axis, up)]
    ppermute x8 -> x0, starting transfers between devices: 9.01 us -> none  [the longest x4 5.28 us: with_halo(): after = lax.ppermute(initial, axis, down)]
    all_gather x1 -> x0, local copies, waits for them, and re-layouts: 7.09 us -> none  [body(): block_piece = lax.all_gather(filtered, 'band', axis=0, tiled=True)]
    dot_general x1 -> x0, matrix products: 4.02 us -> none  [body(): lax.dot_general(panel_rows, flat_piece, (((1,), (1,)), ((), ())), preferr...]
  transfers between devices with their start and end apart: 10 -> 0, of which waited for: 8 -> 0; matrix products, arithmetic and copies ran while one was open for 1% -> 0% of each run, Pallas kernels for 0% -> 0%
where the time goes in v1:
time: 75.4 us; the launch traced here: 75.3 us
  Pallas kernels  67.3 us (89%)
  local copies, waits for them, and re-layouts  7.25 us (10%)
    pallas_call x1, Pallas kernels, body(): pl.pallas_call(functools.partial(kernel, scale), out_shape=(jax.ShapeDtyp...  67.3 us
    reshape x1, local copies, waits for them, and re-layouts, body(): panels.reshape(lines, cells)  3.15 us
    reshape x1, local copies, waits for them, and re-layouts, body(): orbitals.reshape(bands, cells)  2.11 us

profile of v1, /device:TPU:96, one launch (start us, length us, event | category | flops | bytes accessed | tf_op | source)
XLA Modules:
  0.0 75.3 jit_solution(15819651065135834998)
XLA Ops:
  0.6 2.1 %reshape.19.o_ref = bf16[144,2048]{1,0:T(8,128)(2,1)S(1)} reshape(bf16[144,8,2,128]{3,2,1,0:T(2,128)(2,1)} %param.3) | data formatting | bytes 1179648 | tf_op jit(solution)/shard_map/reshape | solution.py:408
  2.7 0.0 copy-start
  2.8 3.1 %reshape.21.p_ref = bf16[288,2048]{1,0:T(8,128)(2,1)S(1)} reshape(bf16[2,144,8,2,128]{4,3,2,1,0:T(2,128)(2,1)} %param.5) | data formatting | bytes 2359296 | tf_op jit(solution)/shard_map/reshape | solution.py:410
  5.9 0.0 copy-done
  5.9 67.3 %shard_map.50 = (bf16[144,2048]{1,0:T(8,128)(2,1)S(1)}, f32[40,288]{1,0:T(8,128)S(1)}) custom-call(bf16[144,2048]{1,0:T(8,128)(2,1)S(1)} %reshape.19.o_ref, f32[16,128]{1,0:T(8,128)S(1)} %bitcast.5, bf16[288,2048]{1,0:T(8,128)(2,1)S(1)} %reshape.21.p_ref), custom_call_target="tpu_custom_call" | custom-call | flops 1358954496 | bytes 4194304 | tf_op jit(solution)/shard_map/pallas_call | solution.py:358
  73.3 1.2 %reshape.22 = bf16[144,8,2,128]{3,2,1,0:T(2,128)(2,1)} reshape(bf16[144,2048]{1,0:T(8,128)(2,1)S(1)} %get-tuple-element.4) | data formatting | bytes 1179648 | tf_op jit(solution)/shard_map/reshape | solution.py:413
  74.5 0.7 reshape.23
  (1 shorter events, 0.0 us)
Async XLA Ops:
  2.7 3.2 %copy-start = (f32[8,2,128]{2,1,0:T(2,128)S(1)}, f32[8,2,128]{2,1,0:T(2,128)}, u32[]{:S(2)}) copy-start(f32[8,2,128]{2,1,0:T(2,128)} %param.4) | copy-start | bytes 24580

commit v2 on v1

--- a/solution.py
+++ b/solution.py
@@ -11,6 +11,7 @@
 MESH = pl.DeviceIdType.MESH
 NT = (((1,), (1,)), ((), ()))
 CHUNKS = ((0, 48), (48, 64), (112, 32))
+PIECE = 48
 
 
 def kernel(
@@ -25,7 +26,13 @@
     xb,
     db,
     pan,
+    edge,
+    lines_of,
+    raw,
+    side,
+    result,
     first,
+    mixed,
     fb,
     core_send,
     core_own,
@@ -33,6 +40,7 @@
     y_send,
     y_recv,
     total,
+    summed,
     z_send,
     z_recv,
     halo_ss,
@@ -40,6 +48,8 @@
     pot_ss,
     pot_rs,
     pan_sem,
+    pan_ss,
+    pan_rs,
     own_sem,
     swap_ss,
     swap_rs,
@@ -73,6 +83,18 @@
     partners += [(gx_ylo, gy, w), (gx_ylo, gy, w_across)]
     for device in partners:
         pl.semaphore_signal(barrier, 1, device_id=device, device_id_type=MESH)
+
+    def spread(src, dst, cell_rows, first_group, groups):
+        def group(i, carry):
+            raw[...] = src[pl.ds(pl.multiple_of(i * 256, 256), 256), :].astype(f32)
+            rows = pl.ds(pl.multiple_of(i * 16, 16), 16)
+            for j, r in enumerate(cell_rows):
+                dst[rows, 128 * j : 128 * (j + 1)] = raw[pl.ds(r, 16, stride=16), :].astype(bf16)
+            return carry
+
+        lax.fori_loop(first_group, first_group + groups, group, 0)
+
+    spread(o_ref, edge, (0, 1, 2, 3, 12, 13, 14, 15), 0, o_ref.shape[0] // 256)
     pl.semaphore_wait(barrier, len(partners))
 
     def remote(src, dst, ss, rs, device):
@@ -93,45 +115,87 @@
             ((gx_next, gy, w), (gx_prev, gy, w), (gx, gy_next, w), (gx, gy_prev, w))
         )
     ]
-    halos = []
-    for k, (s0, n) in enumerate(CHUNKS):
-        rows = pl.ds(s0, n)
-        plan = (
-            (o_ref.at[rows], yb.at[0, rows], (gx, gy_next, w)),
-            (o_ref.at[rows], yb.at[1, rows], (gx, gy_prev, w)),
-            (o_ref.at[rows, pl.ds(1536, 512)], xb.at[0, rows], (gx_next, gy, w)),
-            (o_ref.at[rows, pl.ds(0, 512)], xb.at[1, rows], (gx_prev, gy, w)),
-            (o_ref.at[rows, pl.ds(1920, 128)], db.at[0, rows], (gx_next, gy_next, w)),
-            (o_ref.at[rows, pl.ds(1792, 128)], db.at[1, rows], (gx_next, gy_prev, w)),
-            (o_ref.at[rows, pl.ds(128, 128)], db.at[2, rows], (gx_prev, gy_next, w)),
-            (o_ref.at[rows, pl.ds(0, 128)], db.at[3, rows], (gx_prev, gy_prev, w)),
+    halos = {}
+
+    def send_halo(k, places, plan):
+        for i in places:
+            src, dst, device = plan[i]
+            halos[k, i] = start(remote(src, dst, halo_ss.at[k, i], halo_rs.at[k, i], device))
+
+    def send_layers(k):
+        s0, n = CHUNKS[k]
+        rows = pl.ds(16 * s0, 16 * n)
+        send_halo(
+            k,
+            (0, 1),
+            (
+                (o_ref.at[rows], yb.at[0, rows], (gx, gy_next, w)),
+                (o_ref.at[rows], yb.at[1, rows], (gx, gy_prev, w)),
+            ),
         )
-        halos.append(
-            [
-                start(remote(src, dst, halo_ss.at[k, i], halo_rs.at[k, i], device))
-                for i, (src, dst, device) in enumerate(plan)
-            ]
+
+    def send_edges(k):
+        s0, n = CHUNKS[k]
+        rows = pl.ds(s0, n)
+        send_halo(
+            k,
+            range(2, 8),
+            (
+                None,
+                None,
+                (edge.at[rows, pl.ds(512, 512)], xb.at[0, rows], (gx_next, gy, w)),
+                (edge.at[rows, pl.ds(0, 512)], xb.at[1, rows], (gx_prev, gy, w)),
+                (edge.at[rows, pl.ds(896, 128)], db.at[0, rows], (gx_next, gy_next, w)),
+                (edge.at[rows, pl.ds(768, 128)], db.at[1, rows], (gx_next, gy_prev, w)),
+                (edge.at[rows, pl.ds(128, 128)], db.at[2, rows], (gx_prev, gy_next, w)),
+                (edge.at[rows, pl.ds(0, 128)], db.at[3, rows], (gx_prev, gy_prev, w)),
+            ),
         )
+
+    send_layers(0)
+    send_edges(0)
+    for k in range(1, len(CHUNKS)):
+        send_layers(k)
     mine, theirs = pl.ds(yhi * 1024, 1024), pl.ds(yhi_other * 1024, 1024)
-    pan_own = pltpu.make_async_copy(p_ref.at[:, mine], pan.at[yhi], pan_sem.at[2])
-    pan_own.start()
-    pan_swap = start(
-        remote(p_ref.at[:, theirs], pan.at[yhi], pan_sem.at[0], pan_sem.at[1], (gx, gy, w_across))
-    )
+    panel_swaps = []
+
+    def swap_panels(count):
+        for _ in range(count):
+            i = len(panel_swaps)
+            lines = pl.ds(i * PIECE, PIECE)
+            spread(p_ref, lines_of, range(16), i * (PIECE // 16), PIECE // 16)
+            panel_swaps.append(
+                start(
+                    remote(
+                        lines_of.at[lines, theirs],
+                        pan.at[yhi, lines],
+                        pan_ss.at[i],
+                        pan_rs.at[i],
+                        (gx, gy, w_across),
+                    )
+                )
+            )
+
+    swap_panels(2)
     z_send[:, 32:48, :] = jnp.zeros((8, 16, z_send.shape[2]), bf16)
 
-    def filter_rows(rows):
+    def filter_rows(i):
+        rows = pl.ds(pl.multiple_of(i * 16, 16), 16)
+        stored = pl.ds(pl.multiple_of(i * 256, 256), 256)
+        raw[...] = o_ref[stored, :].astype(f32)
+        for d in range(2):
+            side[d] = yb[d, stored, :].astype(f32)
+
         def orb(x, y):
             if 0 <= x < 8:
                 if y < 0:
-                    piece = yb[0, rows, 128 * (2 * x + y + 2) : 128 * (2 * x + y + 3)]
-                elif y > 1:
-                    piece = yb[1, rows, 128 * (2 * x + y - 2) : 128 * (2 * x + y - 1)]
-                else:
-                    piece = o_ref[rows, 128 * (2 * x + y) : 128 * (2 * x + y + 1)]
-            elif 0 <= y < 2:
-                side, r = (0, 2 * (x + 2) + y) if x < 0 else (1, 2 * (x - 8) + y)
-                piece = xb[side, rows, 128 * r : 128 * (r + 1)]
+                    return side[0, pl.ds(2 * x + y + 2, 16, stride=16), :]
+                if y > 1:
+                    return side[1, pl.ds(2 * x + y - 2, 16, stride=16), :]
+                return raw[pl.ds(2 * x + y, 16, stride=16), :]
+            if 0 <= y < 2:
+                d, r = (0, 2 * (x + 2) + y) if x < 0 else (1, 2 * (x - 8) + y)
+                piece = xb[d, rows, 128 * r : 128 * (r + 1)]
             else:
                 piece = db[(0 if x < 0 else 2) + (0 if y < 0 else 1), rows, :]
             return piece.astype(f32)
@@ -170,7 +234,9 @@
                 s = s + first[slot(x, y + 1)] + first[slot(x, y - 1)]
                 value = 2.0 * coefficient(x, y) * v - s * (1.0 / 3.0) - orb(x, y)
                 r = 2 * x + y
-                filt_ref[rows, 128 * r : 128 * (r + 1)] = value.astype(bf16)
+                result[pl.ds(r, 16, stride=16), :] = value
+                mixed[rows, 128 * r : 128 * (r + 1)] = value.astype(bf16)
+        filt_ref[stored, :] = result[...].astype(bf16)
 
     swaps, owns, near, far = {}, {}, {}, {}
     cores, ys, zs = {}, {}, []
@@ -180,31 +246,31 @@
         if k == 0:
             for copy in pots:
                 copy.wait_recv()
-        for copy in halos[k]:
-            copy.wait_recv()
+        for i in range(8):
+            halos[k, i].wait_recv()
 
         def sub(i, carry):
-            filter_rows(pl.ds(pl.multiple_of(s0 + i * 16, 16), 16))
+            filter_rows(s0 // 16 + i)
             return carry
 
         lax.fori_loop(0, n // 16, sub, 0)
         rows = pl.ds(s0, n)
         swaps[k] = start(
             remote(
-                filt_ref.at[rows, theirs], fb.at[w, rows], swap_ss.at[k], swap_rs.at[k], (gx, gy, w_across)
+                mixed.at[rows, theirs], fb.at[w, rows], swap_ss.at[k], swap_rs.at[k], (gx, gy, w_across)
             )
         )
         for d, to in enumerate((w_next, w_prev)):
             near[k, 0, d] = start(
                 remote(
-                    filt_ref.at[rows, mine],
+                    mixed.at[rows, mine],
                     fb.at[w, rows],
                     near_ss.at[k, 0, d],
                     near_rs.at[k, 0, d],
                     (gx, gy, to),
                 )
             )
-        owns[k] = pltpu.make_async_copy(filt_ref.at[rows, mine], fb.at[w, rows], own_sem.at[k])
+        owns[k] = pltpu.make_async_copy(mixed.at[rows, mine], fb.at[w, rows], own_sem.at[k])
         owns[k].start()
 
     def step_swap(k):
@@ -237,8 +303,11 @@
         s0, n = CHUNKS[k]
         rows = pl.ds(s0, n)
         if k == 0:
+            pan_own = pltpu.make_async_copy(lines_of.at[:, mine], pan.at[yhi], pan_sem.at[0])
+            pan_own.start()
             pan_own.wait()
-            pan_swap.wait_recv()
+            for copy in panel_swaps:
+                copy.wait_recv()
         owns[k].wait()
         for t in range(2):
             for d in range(2):
@@ -302,7 +371,7 @@
 
                 @pl.when(target == gy)
                 def _():
-                    out_ref[0:36, :] = block
+                    summed[0:36, :] = block
 
                 @pl.when(target != gy)
                 def _():
@@ -311,27 +380,28 @@
                         z_send.at[target], z_recv.at[gy], z_ss.at[target], z_rs.at[gy], (gx, target, w)
                     ).start()
 
-    step_filter(0)
-    step_swap(0)
-    step_forward(0, 0)
-    step_filter(1)
-    step_forward(0, 1)
-    step_swap(1)
+    last = len(CHUNKS) - 1
+    for k in range(last + 1):
+        step_filter(k)
+        if k < last:
+            send_edges(k + 1)
+        swap_panels((2, 2, 0)[k])
+        if k > 0:
+            step_forward(k - 1, 1)
+        step_swap(k)
+        if k < last:
+            step_forward(k, 0)
     step_matmul(0)
-    step_forward(1, 0)
-    step_filter(2)
-    step_forward(1, 1)
-    step_swap(2)
+    step_forward(last, 0)
     step_core(0)
     step_matmul(1)
-    step_forward(2, 0)
+    step_forward(last, 1)
     step_core(1)
-    step_forward(2, 1)
+    step_matmul(last)
     step_y(0)
+    step_core(last)
     step_y(1)
-    step_matmul(2)
-    step_core(2)
-    step_y(2)
+    step_y(last)
 
     for s in range(8):
 
@@ -339,9 +409,12 @@
         def _():
             copy = remote(z_send.at[s], z_recv.at[s], z_ss.at[s], z_rs.at[s], (gx, s, w))
             copy.wait_recv()
-            out_ref[0:36, :] += z_recv[s, 0:36, :].astype(f32)
+            summed[0:36, :] += z_recv[s, 0:36, :].astype(f32)
             copy.wait_send()
 
+    lanes = out_ref.shape[2]
+    for p in range(2):
+        out_ref[:, p, :] = summed[0:36, lanes * p : lanes * (p + 1)]
     for copy in pending:
         copy.wait_send()
 
@@ -358,18 +431,24 @@
     filtered, sums = pl.pallas_call(
         functools.partial(kernel, scale),
         out_shape=(
-            jax.ShapeDtypeStruct((bands, cells), bf16),
-            jax.ShapeDtypeStruct((40, lines), f32),
+            jax.ShapeDtypeStruct((bands * lx * ly, lz), bf16),
+            jax.ShapeDtypeStruct((36, panel_count, bands), f32),
         ),
         in_specs=[pl.BlockSpec(memory_space=pltpu.VMEM)] * 3,
         out_specs=(pl.BlockSpec(memory_space=pltpu.VMEM),) * 2,
         scratch_shapes=[
             pltpu.VMEM((4, lx * ly, lz), f32),
-            pltpu.VMEM((2, bands, cells), bf16),
+            pltpu.VMEM((2, bands * lx * ly, lz), bf16),
             pltpu.VMEM((2, bands, 512), bf16),
             pltpu.VMEM((4, bands, 128), bf16),
             pltpu.VMEM((2, lines, cells // 2), bf16),
+            pltpu.VMEM((bands, 1024), bf16),
+            pltpu.VMEM((lines, cells), bf16),
+            pltpu.VMEM((256, lz), f32),
+            pltpu.VMEM((2, 256, lz), f32),
+            pltpu.VMEM((256, lz), f32),
             pltpu.VMEM((36, 16, 128), f32),
+            pltpu.VMEM((bands, cells), bf16),
             pltpu.VMEM((8, bands, cells // 2), bf16),
             pltpu.VMEM((2, 2, 2, bands, lines), f32),
             pltpu.VMEM((2, 2, 2, bands, lines), f32),
@@ -377,13 +456,16 @@
             pltpu.VMEM((3, 2, bands, lines), bf16),
             pltpu.VMEM((3, 2, bands, lines), bf16),
             pltpu.VMEM((2, bands, lines), f32),
+            pltpu.VMEM((40, lines), f32),
             pltpu.VMEM((8, 48, lines), bf16),
             pltpu.VMEM((8, 48, lines), bf16),
             dma((c, 8)),
             dma((c, 8)),
             dma((4,)),
             dma((4,)),
-            dma((3,)),
+            dma((1,)),
+            dma((6,)),
+            dma((6,)),
             dma((c,)),
             dma((c,)),
             dma((c,)),
@@ -405,11 +487,11 @@
             flops=2 * lines * bands * 8 * cells, bytes_accessed=4 << 20, transcendentals=0
         ),
     )(
-        orbitals.reshape(bands, cells),
+        orbitals.reshape(bands * lx * ly, lz),
         potential.reshape(lx * ly, lz),
-        panels.reshape(lines, cells),
+        panels.reshape(lines * lx * ly, lz),
     )
-    margin = sums[:36].T.reshape(panel_count, bands, 36)
+    margin = sums.transpose(1, 2, 0)
     return filtered.reshape(orbitals.shape), margin
 
 

time: 75.4 us -> 65.8 us (0.87); the launches traced: 75.3 us -> 64.8 us
  Pallas kernels: 67.3 us -> 59.6 us
  local copies, waits for them, and re-layouts: 7.25 us -> 4.47 us
    pallas_call x1, Pallas kernels: 67.3 us -> 59.6 us  [body(): pl.pallas_call(functools.partial(kernel, scale), out_shape=(jax.ShapeDtyp...]
    reshape x4 -> x0, local copies, waits for them, and re-layouts: 7.23 us -> none  [the longest x1 3.15 us: body(): panels.reshape(lines, cells)]
    unnamed x2 -> x8, local copies, waits for them, and re-layouts: 0.01 us -> 4.47 us
where the time goes in v2:
time: 65.8 us; the launch traced here: 64.8 us
  Pallas kernels  59.6 us (91%)
  local copies, waits for them, and re-layouts  4.47 us (7%)
    pallas_call x1, Pallas kernels, body(): pl.pallas_call(functools.partial(kernel, scale), out_shape=(jax.ShapeDtyp...  59.6 us
    unnamed x8, local copies, waits for them, and re-layouts  4.47 us

profile of v2, /device:TPU:96, one launch (start us, length us, event | category | flops | bytes accessed | tf_op | source)
XLA Modules:
  0.0 64.8 jit_solution(4831819975619072213)
XLA Ops:
  0.6 0.0 copy-start
  0.6 1.3 %copy-done = bf16[2,144,8,2,128]{4,3,2,1,0:T(2,128)(2,1)S(1)} copy-done((bf16[2,144,8,2,128]{4,3,2,1,0:T(2,128)(2,1)S(1)}, bf16[2,144,8,2,128]{4,3,2,1,0:T(2,128)(2,1)}, u32[]{:S(2)}) %copy-start) | copy-done | bytes 1179672
  1.9 0.0 copy-start.1
  1.9 1.1 %copy-done.1 = bf16[144,8,2,128]{3,2,1,0:T(2,128)(2,1)S(1)} copy-done((bf16[144,8,2,128]{3,2,1,0:T(2,128)(2,1)S(1)}, bf16[144,8,2,128]{3,2,1,0:T(2,128)(2,1)}, u32[]{:S(2)}) %copy-start.1) | copy-done | bytes 589848
  3.0 0.0 copy-start.2
  3.0 0.7 %copy-done.2 = f32[8,2,128]{2,1,0:T(2,128)S(1)} copy-done((f32[8,2,128]{2,1,0:T(2,128)S(1)}, f32[8,2,128]{2,1,0:T(2,128)}, u32[]{:S(2)}) %copy-start.2) | copy-done | bytes 8216
  3.7 59.6 %shard_map.50 = (bf16[2304,128]{1,0:T(8,128)(2,1)S(1)}, f32[36,2,144]{2,1,0:T(2,128)S(1)}) custom-call(bf16[2304,128]{1,0:T(8,128)(2,1)S(1)} %bitcast.8, f32[16,128]{1,0:T(8,128)S(1)} %bitcast.9, bf16[4608,128]{1,0:T(8,128)(2,1)S(1)} %bitcast.7), custom_call_target="tpu_custom_call" | custom-call | flops 1358954496 | bytes 4194304 | tf_op jit(solution)/shard_map/pallas_call | solution.py:431
  63.3 0.8 %copy.7 = bf16[144,8,2,128]{3,2,1,0:T(2,128)(2,1)} copy(bf16[144,8,2,128]{3,2,1,0:T(2,128)(2,1)S(1)} %bitcast.5) | data formatting | bytes 1179648
  64.1 0.6 copy.8
Async XLA Ops:
  0.6 1.3 %copy-start = (bf16[2,144,8,2,128]{4,3,2,1,0:T(2,128)(2,1)S(1)}, bf16[2,144,8,2,128]{4,3,2,1,0:T(2,128)(2,1)}, u32[]{:S(2)}) copy-start(bf16[2,144,8,2,128]{4,3,2,1,0:T(2,128)(2,1)} %param.5) | copy-start | bytes 3538948
  1.9 1.1 %copy-start.1 = (bf16[144,8,2,128]{3,2,1,0:T(2,128)(2,1)S(1)}, bf16[144,8,2,128]{3,2,1,0:T(2,128)(2,1)}, u32[]{:S(2)}) copy-start(bf16[144,8,2,128]{3,2,1,0:T(2,128)(2,1)} %param.3) | copy-start | bytes 1769476
  3.0 0.7 %copy-start.2 = (f32[8,2,128]{2,1,0:T(2,128)S(1)}, f32[8,2,128]{2,1,0:T(2,128)}, u32[]{:S(2)}) copy-start(f32[8,2,128]{2,1,0:T(2,128)} %param.4) | copy-start | bytes 24580

commit v3 on v2

--- a/solution.py
+++ b/solution.py
@@ -68,18 +68,22 @@
     gx, gy, w = lax.axis_index("gx"), lax.axis_index("gy"), lax.axis_index("band")
     ylo, core = gx // 2, gx % 2
     yhi, xx = w // 4, w % 4
-    ylo_other, core_other, yhi_other = 1 - ylo, 1 - core, 1 - yhi
+    ylo_other, core_other = 1 - ylo, 1 - core
+    half = (xx // 2 + xx) % 2
+    half_other = 1 - half
     gx_prev, gx_next = (gx + 3) % 4, (gx + 1) % 4
     gy_prev, gy_next = (gy + 7) % 8, (gy + 1) % 8
-    w_next, w_prev = yhi * 4 + (xx + 1) % 4, yhi * 4 + (xx + 3) % 4
-    w_across = yhi_other * 4 + xx
+    xx_across = xx + 1 - 2 * (xx % 2)
+    w_across = yhi * 4 + xx_across
+    w_near = ((1 - yhi) * 4 + xx, yhi * 4 + 3 - xx)
+    w_near_across = ((1 - yhi) * 4 + xx_across, yhi * 4 + 3 - xx_across)
     gx_core, gx_ylo = ylo * 2 + core_other, ylo_other * 2 + core
 
     barrier = pltpu.get_barrier_semaphore()
     partners = [(gx_prev, gy, w), (gx_next, gy, w)]
     partners += [(gx, (gy + d) % 8, w) for d in range(1, 8)]
     partners += [(a, b, w) for a in (gx_prev, gx_next) for b in (gy_prev, gy_next)]
-    partners += [(gx, gy, w_across), (gx, gy, w_next), (gx, gy, w_prev)]
+    partners += [(gx, gy, w_across), (gx, gy, w_near[0]), (gx, gy, w_near[1])]
     partners += [(gx_ylo, gy, w), (gx_ylo, gy, w_across)]
     for device in partners:
         pl.semaphore_signal(barrier, 1, device_id=device, device_id_type=MESH)
@@ -156,7 +160,7 @@
     send_edges(0)
     for k in range(1, len(CHUNKS)):
         send_layers(k)
-    mine, theirs = pl.ds(yhi * 1024, 1024), pl.ds(yhi_other * 1024, 1024)
+    mine, theirs = pl.ds(half * 1024, 1024), pl.ds(half_other * 1024, 1024)
     panel_swaps = []
 
     def swap_panels(count):
@@ -168,7 +172,7 @@
                 start(
                     remote(
                         lines_of.at[lines, theirs],
-                        pan.at[yhi, lines],
+                        pan.at[half, lines],
                         pan_ss.at[i],
                         pan_rs.at[i],
                         (gx, gy, w_across),
@@ -260,7 +264,7 @@
                 mixed.at[rows, theirs], fb.at[w, rows], swap_ss.at[k], swap_rs.at[k], (gx, gy, w_across)
             )
         )
-        for d, to in enumerate((w_next, w_prev)):
+        for d, to in enumerate(w_near):
             near[k, 0, d] = start(
                 remote(
                     mixed.at[rows, mine],
@@ -277,7 +281,7 @@
         s0, n = CHUNKS[k]
         rows = pl.ds(s0, n)
         swaps[k].wait_recv()
-        for d, to in enumerate((w_next, w_prev)):
+        for d, to in enumerate(w_near):
             near[k, 1, d] = start(
                 remote(
                     fb.at[w_across, rows],
@@ -291,10 +295,10 @@
     def step_forward(k, t):
         s0, n = CHUNKS[k]
         rows = pl.ds(s0, n)
-        half = yhi if t == 0 else yhi_other
-        for d, (to, origin) in enumerate(((w_next, (xx + 3) % 4), (w_prev, (xx + 1) % 4))):
+        for d, origin in enumerate(w_near if t == 0 else w_near_across):
+            to = w_near[1 - d]
             near[k, t, d].wait_recv()
-            piece = fb.at[half * 4 + origin, rows, pl.ds(512 * d, 512)]
+            piece = fb.at[origin, rows, pl.ds(512 * d, 512)]
             far[k, t, d] = start(
                 remote(piece, piece, far_ss.at[k, t, d], far_rs.at[k, t, d], (gx, gy, to))
             )
@@ -303,7 +307,7 @@
         s0, n = CHUNKS[k]
         rows = pl.ds(s0, n)
         if k == 0:
-            pan_own = pltpu.make_async_copy(lines_of.at[:, mine], pan.at[yhi], pan_sem.at[0])
+            pan_own = pltpu.make_async_copy(lines_of.at[:, mine], pan.at[half], pan_sem.at[0])
             pan_own.start()
             pan_own.wait()
             for copy in panel_swaps:
@@ -332,9 +336,9 @@
                 )
 
     y_plan = (
-        (ylo_other, yhi, (gx_ylo, gy, w)),
-        (ylo, yhi_other, (gx, gy, w_across)),
-        (ylo_other, yhi_other, (gx_ylo, gy, w_across)),
+        (ylo_other, half, (gx_ylo, gy, w)),
+        (ylo, half_other, (gx, gy, w_across)),
+        (ylo_other, half_other, (gx_ylo, gy, w_across)),
     )
 
     def step_core(k):
@@ -351,7 +355,7 @@
                 )
             )
         for q in range(2):
-            total[q, rows, :] = core_own[ylo, q, yhi, rows, :] + core_recv[ylo, q, yhi, rows, :]
+            total[q, rows, :] = core_own[ylo, q, half, rows, :] + core_recv[ylo, q, half, rows, :]
 
     def step_y(k):
         s0, n = CHUNKS[k]

time: 65.8 us -> 64.4 us (0.979); the launches traced: 64.8 us -> 64.2 us
  no operation moved by 1% of the time
where the time goes in v3:
time: 64.4 us; the launch traced here: 64.2 us
  Pallas kernels  59 us (92%)
  local copies, waits for them, and re-layouts  4.47 us (7%)
  between operations  0.65 us (1%)
    pallas_call x1, Pallas kernels, body(): pl.pallas_call(functools.partial(kernel, scale), out_shape=(jax.ShapeDtyp...  59 us
    unnamed x8, local copies, waits for them, and re-layouts  4.47 us

profile of v3, /device:TPU:96, one launch (start us, length us, event | category | flops | bytes accessed | tf_op | source)
XLA Modules:
  0.0 64.2 jit_solution(10626489171055083891)
XLA Ops:
  0.6 0.0 copy-start
  0.6 1.3 %copy-done = bf16[2,144,8,2,128]{4,3,2,1,0:T(2,128)(2,1)S(1)} copy-done((bf16[2,144,8,2,128]{4,3,2,1,0:T(2,128)(2,1)S(1)}, bf16[2,144,8,2,128]{4,3,2,1,0:T(2,128)(2,1)}, u32[]{:S(2)}) %copy-start) | copy-done | bytes 1179672
  1.9 0.0 copy-start.1
  1.9 1.1 %copy-done.1 = bf16[144,8,2,128]{3,2,1,0:T(2,128)(2,1)S(1)} copy-done((bf16[144,8,2,128]{3,2,1,0:T(2,128)(2,1)S(1)}, bf16[144,8,2,128]{3,2,1,0:T(2,128)(2,1)}, u32[]{:S(2)}) %copy-start.1) | copy-done | bytes 589848
  3.0 0.0 copy-start.2
  3.0 0.7 %copy-done.2 = f32[8,2,128]{2,1,0:T(2,128)S(1)} copy-done((f32[8,2,128]{2,1,0:T(2,128)S(1)}, f32[8,2,128]{2,1,0:T(2,128)}, u32[]{:S(2)}) %copy-start.2) | copy-done | bytes 8216
  3.7 59.0 %shard_map.50 = (bf16[2304,128]{1,0:T(8,128)(2,1)S(1)}, f32[36,2,144]{2,1,0:T(2,128)S(1)}) custom-call(bf16[2304,128]{1,0:T(8,128)(2,1)S(1)} %bitcast.8, f32[16,128]{1,0:T(8,128)S(1)} %bitcast.9, bf16[4608,128]{1,0:T(8,128)(2,1)S(1)} %bitcast.7), custom_call_target="tpu_custom_call" | custom-call | flops 1358954496 | bytes 4194304 | tf_op jit(solution)/shard_map/pallas_call | solution.py:435
  62.7 0.8 %copy.7 = bf16[144,8,2,128]{3,2,1,0:T(2,128)(2,1)} copy(bf16[144,8,2,128]{3,2,1,0:T(2,128)(2,1)S(1)} %bitcast.5) | data formatting | bytes 1179648
  63.5 0.6 copy.8
Async XLA Ops:
  0.6 1.3 %copy-start = (bf16[2,144,8,2,128]{4,3,2,1,0:T(2,128)(2,1)S(1)}, bf16[2,144,8,2,128]{4,3,2,1,0:T(2,128)(2,1)}, u32[]{:S(2)}) copy-start(bf16[2,144,8,2,128]{4,3,2,1,0:T(2,128)(2,1)} %param.5) | copy-start | bytes 3538948
  1.9 1.1 %copy-start.1 = (bf16[144,8,2,128]{3,2,1,0:T(2,128)(2,1)S(1)}, bf16[144,8,2,128]{3,2,1,0:T(2,128)(2,1)}, u32[]{:S(2)}) copy-start(bf16[144,8,2,128]{3,2,1,0:T(2,128)(2,1)} %param.3) | copy-start | bytes 1769476
  3.0 0.7 %copy-start.2 = (f32[8,2,128]{2,1,0:T(2,128)S(1)}, f32[8,2,128]{2,1,0:T(2,128)}, u32[]{:S(2)}) copy-start(f32[8,2,128]{2,1,0:T(2,128)} %param.4) | copy-start | bytes 24580

commit v4 on v3

--- a/solution.py
+++ b/solution.py
@@ -16,11 +16,15 @@
 
 def kernel(
     scale,
+    o_hbm,
+    pot_hbm,
+    p_hbm,
+    filt_ref,
+    out_ref,
     o_ref,
     pot_ref,
     p_ref,
-    filt_ref,
-    out_ref,
+    load_sem,
     potn,
     yb,
     xb,
@@ -79,6 +83,12 @@
     w_near_across = ((1 - yhi) * 4 + xx_across, yhi * 4 + 3 - xx_across)
     gx_core, gx_ylo = ylo * 2 + core_other, ylo_other * 2 + core
 
+    loads = [
+        pltpu.make_async_copy(src, dst, load_sem.at[i])
+        for i, (src, dst) in enumerate(((o_hbm, o_ref), (pot_hbm, pot_ref), (p_hbm, p_ref)))
+    ]
+    for copy in loads:
+        copy.start()
     barrier = pltpu.get_barrier_semaphore()
     partners = [(gx_prev, gy, w), (gx_next, gy, w)]
     partners += [(gx, (gy + d) % 8, w) for d in range(1, 8)]
@@ -98,7 +108,9 @@
 
         lax.fori_loop(first_group, first_group + groups, group, 0)
 
+    loads[0].wait()
     spread(o_ref, edge, (0, 1, 2, 3, 12, 13, 14, 15), 0, o_ref.shape[0] // 256)
+    loads[1].wait()
     pl.semaphore_wait(barrier, len(partners))
 
     def remote(src, dst, ss, rs, device):
@@ -133,8 +145,8 @@
             k,
             (0, 1),
             (
-                (o_ref.at[rows], yb.at[0, rows], (gx, gy_next, w)),
-                (o_ref.at[rows], yb.at[1, rows], (gx, gy_prev, w)),
+                (o_hbm.at[rows], yb.at[0, rows], (gx, gy_next, w)),
+                (o_hbm.at[rows], yb.at[1, rows], (gx, gy_prev, w)),
             ),
         )
 
@@ -180,6 +192,7 @@
                 )
             )
 
+    loads[2].wait()
     swap_panels(2)
     z_send[:, 32:48, :] = jnp.zeros((8, 16, z_send.shape[2]), bf16)
 
@@ -438,9 +451,13 @@
             jax.ShapeDtypeStruct((bands * lx * ly, lz), bf16),
             jax.ShapeDtypeStruct((36, panel_count, bands), f32),
         ),
-        in_specs=[pl.BlockSpec(memory_space=pltpu.VMEM)] * 3,
+        in_specs=[pl.BlockSpec(memory_space=pltpu.HBM)] * 3,
         out_specs=(pl.BlockSpec(memory_space=pltpu.VMEM),) * 2,
         scratch_shapes=[
+            pltpu.VMEM((bands * lx * ly, lz), bf16),
+            pltpu.VMEM((lx * ly, lz), f32),
+            pltpu.VMEM((lines * lx * ly, lz), bf16),
+            dma((3,)),
             pltpu.VMEM((4, lx * ly, lz), f32),
             pltpu.VMEM((2, bands * lx * ly, lz), bf16),
             pltpu.VMEM((2, bands, 512), bf16),
@@ -485,7 +502,7 @@
             dma((8,)),
         ],
         compiler_params=pltpu.CompilerParams(
-            collective_id=0, has_side_effects=True, vmem_limit_bytes=48 << 20
+            collective_id=0, has_side_effects=True, vmem_limit_bytes=62 << 20
         ),
         cost_estimate=pl.CostEstimate(
             flops=2 * lines * bands * 8 * cells, bytes_accessed=4 << 20, transcendentals=0

time: 64.4 us -> 63.8 us (level)
  local copies, waits for them, and re-layouts: 4.47 us -> 2.95 us
  Pallas kernels: 59 us -> 60.1 us
    unnamed x8 -> x4, local copies, waits for them, and re-layouts: 4.47 us -> 2.95 us
    pallas_call x1, Pallas kernels: 59 us -> 60.1 us  [body(): pl.pallas_call(functools.partial(kernel, scale), out_shape=(jax.ShapeDtyp...]
where the time goes in v4:
time: 63.8 us; the launch traced here: 63.7 us
  Pallas kernels  60.1 us (94%)
  local copies, waits for them, and re-layouts  2.95 us (5%)
  between operations  0.65 us (1%)
    pallas_call x1, Pallas kernels, body(): pl.pallas_call(functools.partial(kernel, scale), out_shape=(jax.ShapeDtyp...  60.1 us
    unnamed x4, local copies, waits for them, and re-layouts  2.95 us

profile of v4, /device:TPU:96, one launch (start us, length us, event | category | flops | bytes accessed | tf_op | source)
XLA Modules:
  0.0 63.7 jit_solution(8093891200857268765)
XLA Ops:
  0.6 60.1 %shard_map.50 = (bf16[2304,128]{1,0:T(8,128)(2,1)}, f32[36,2,144]{2,1,0:T(2,128)}) custom-call(bf16[2304,128]{1,0:T(8,128)(2,1)} %bitcast.8, f32[16,128]{1,0:T(8,128)} %bitcast.9, bf16[4608,128]{1,0:T(8,128)(2,1)} %bitcast.7), custom_call_target="tpu_custom_call" | custom-call | flops 1358954496 | bytes 4194304 | tf_op jit(solution)/shard_map/pallas_call | solution.py:448
  60.8 0.0 copy-start
  60.8 2.3 %copy.7 = bf16[144,8,2,128]{3,2,1,0:T(2,128)(2,1)} copy(bf16[144,8,2,128]{3,2,1,0:T(2,128)(2,1)} %bitcast.5) | data formatting | bytes 1179648
  63.1 0.0 copy-done
  63.1 0.6 copy.8
Async XLA Ops:
  60.8 2.3 %copy-start = (f32[36,2,144]{2,1,0:T(2,128)S(1)}, f32[36,2,144]{2,1,0:T(2,128)}, u32[]{:S(2)}) copy-start(f32[36,2,144]{2,1,0:T(2,128)} %get-tuple-element.5) | copy-start | bytes 124420

commit v5 on v4

--- a/solution.py
+++ b/solution.py
@@ -170,8 +170,9 @@
 
     send_layers(0)
     send_edges(0)
-    for k in range(1, len(CHUNKS)):
-        send_layers(k)
+    send_layers(1)
+    send_edges(1)
+    send_layers(2)
     mine, theirs = pl.ds(half * 1024, 1024), pl.ds(half_other * 1024, 1024)
     panel_swaps = []
 
@@ -400,8 +401,8 @@
     last = len(CHUNKS) - 1
     for k in range(last + 1):
         step_filter(k)
-        if k < last:
-            send_edges(k + 1)
+        if k == 0:
+            send_edges(2)
         swap_panels((2, 2, 0)[k])
         if k > 0:
             step_forward(k - 1, 1)

time: 63.8 us -> 63.2 us (level)
  Pallas kernels: 60.1 us -> 59.1 us
    pallas_call x1, Pallas kernels: 60.1 us -> 59.1 us  [body(): pl.pallas_call(functools.partial(kernel, scale), out_shape=(jax.ShapeDtyp...]
where the time goes in v5:
time: 63.2 us; the launch traced here: 62.7 us
  Pallas kernels  59.1 us (94%)
  local copies, waits for them, and re-layouts  2.95 us (5%)
  between operations  0.65 us (1%)
    pallas_call x1, Pallas kernels, body(): pl.pallas_call(functools.partial(kernel, scale), out_shape=(jax.ShapeDtyp...  59.1 us
    unnamed x4, local copies, waits for them, and re-layouts  2.95 us

profile of v5, /device:TPU:96, one launch (start us, length us, event | category | flops | bytes accessed | tf_op | source)
XLA Modules:
  0.0 62.7 jit_solution(9037855190539881061)
XLA Ops:
  0.6 59.1 %shard_map.50 = (bf16[2304,128]{1,0:T(8,128)(2,1)}, f32[36,2,144]{2,1,0:T(2,128)}) custom-call(bf16[2304,128]{1,0:T(8,128)(2,1)} %bitcast.8, f32[16,128]{1,0:T(8,128)} %bitcast.9, bf16[4608,128]{1,0:T(8,128)(2,1)} %bitcast.7), custom_call_target="tpu_custom_call" | custom-call | flops 1358954496 | bytes 4194304 | tf_op jit(solution)/shard_map/pallas_call | solution.py:449
  59.7 0.0 copy-start
  59.8 2.3 %copy.7 = bf16[144,8,2,128]{3,2,1,0:T(2,128)(2,1)} copy(bf16[144,8,2,128]{3,2,1,0:T(2,128)(2,1)} %bitcast.5) | data formatting | bytes 1179648
  62.1 0.0 copy-done
  62.1 0.6 %copy.8 = f32[2,144,36]{1,0,2:T(2,128)} copy(f32[2,144,36]{1,0,2:T(2,128)S(1)} %bitcast.6) | data formatting | bytes 82944
Async XLA Ops:
  59.7 2.3 %copy-start = (f32[36,2,144]{2,1,0:T(2,128)S(1)}, f32[36,2,144]{2,1,0:T(2,128)}, u32[]{:S(2)}) copy-start(f32[36,2,144]{2,1,0:T(2,128)} %get-tuple-element.5) | copy-start | bytes 124420
